TPU v7x, 32 devices: a whole 2x2x4 slice. The times are simulated.
32 devices in a mesh: tm: 16 (over z, y, x), space: 2 (over core).
Axes of the slice: x: 2, y: 2, z: 4, core: 2. Of those that a mesh axis runs over, the one named last changes fastest.
Arguments:
- snapshots: float32 [4096, 3, 1024], P('tm', None, 'space'), may hold values from -108 to 108
- weights: float32 [1024], P('space'), may hold values from 0.1 to 1
- start: float32 [2, 15, 8], replicated, may hold values from -6 to 6
Outputs:
- mode_out: float32 [64, 8, 2, 3, 1024], P('tm', None, None, None, 'space')
- energy: float32 [64, 8], P('tm')
All inputs are finite; a program needn't handle non-finite values.
Results may differ from a plain program's by a relative error of at most 0.0003.
Values sent between devices are 32-bit elements; how exact they have to be, the bound alone decides.
A program may use at most 64 MiB of HBM per device.

v0:
```python
import math
import jax
import jax.numpy as jnp
from jax import lax
from jax.sharding import PartitionSpec as P

NF = 64
ITERS = 8
precise = lax.Precision.HIGHEST
epsilon = 1e-06


def shifted(block, axis, distance):
    devices = range(lax.axis_size(axis))
    route = [(i - distance, i) for i in devices if i - distance in devices]
    return lax.ppermute(block, axis, route)


def dft_table(freqs, seg_len):
    length = 2 * seg_len
    times = jnp.arange(length, dtype=jnp.int32)
    freq_ids = jnp.arange(freqs, dtype=jnp.int32)
    turns = jnp.mod(freq_ids[:, None] * times[None, :], length).astype(jnp.float32)
    phase = 2.0 * math.pi / length * turns
    window = 0.5 - 0.5 * jnp.cos(2.0 * math.pi / length * times.astype(jnp.float32))
    factor = 1.0 / jnp.sqrt(jnp.sum(window * window))
    return jnp.concatenate([window * jnp.cos(phase) * factor, -window * jnp.sin(phase) * factor], 0)


def gram_parts(spectra, col_weights, total_points):
    weighted = spectra * col_weights
    grams = jnp.einsum("nrfc,msfc->frnsm", spectra, weighted, precision=precise)
    gram_re = (grams[:, 0, :, 0, :] + grams[:, 1, :, 1, :]) / total_points
    gram_im = (grams[:, 0, :, 1, :] - grams[:, 1, :, 0, :]) / total_points
    return (gram_re, gram_im)


def apply_gram(gram_re, gram_im, vec_re, vec_im):
    img_re = jnp.einsum("fnm,fmk->fnk", gram_re, vec_re, precision=precise) - jnp.einsum(
        "fnm,fmk->fnk", gram_im, vec_im, precision=precise
    )
    img_im = jnp.einsum("fnm,fmk->fnk", gram_re, vec_im, precision=precise) + jnp.einsum(
        "fnm,fmk->fnk", gram_im, vec_re, precision=precise
    )
    return (img_re, img_im)


def orthonormal(img_re, img_im):
    cols_re = []
    cols_im = []
    for column in range(img_re.shape[-1]):
        part_re = img_re[..., column]
        part_im = img_im[..., column]
        if column > 0:
            prev_re = jnp.stack(cols_re, -1)
            prev_im = jnp.stack(cols_im, -1)
            for repeat in range(2):
                coef_re = jnp.sum(
                    prev_re * part_re[..., None] + prev_im * part_im[..., None], axis=1
                )
                coef_im = jnp.sum(
                    prev_re * part_im[..., None] - prev_im * part_re[..., None], axis=1
                )
                part_re = part_re - jnp.sum(
                    prev_re * coef_re[:, None, :] - prev_im * coef_im[:, None, :], axis=-1
                )
                part_im = part_im - jnp.sum(
                    prev_re * coef_im[:, None, :] + prev_im * coef_re[:, None, :], axis=-1
                )
        inverse = 1.0 / jnp.sqrt(jnp.sum(part_re * part_re + part_im * part_im, axis=1) + epsilon)
        cols_re.append(part_re * inverse[:, None])
        cols_im.append(part_im * inverse[:, None])
    return (jnp.stack(cols_re, -1), jnp.stack(cols_im, -1))


def subspace(gram_re, gram_im, start):
    shape = (gram_re.shape[0], start.shape[1], start.shape[2])
    vec_re = jnp.broadcast_to(start[0], shape)
    vec_im = jnp.broadcast_to(start[1], shape)
    for sweep in range(ITERS):
        img_re, img_im = apply_gram(gram_re, gram_im, vec_re, vec_im)
        vec_re, vec_im = orthonormal(img_re, img_im)
    return (vec_re, vec_im)


def project(spectra, vec_re, vec_im):
    real_rows = spectra[:, 0]
    imag_rows = spectra[:, 1]
    mode_re = jnp.einsum("nfc,fnk->fkc", real_rows, vec_re, precision=precise) - jnp.einsum(
        "nfc,fnk->fkc", imag_rows, vec_im, precision=precise
    )
    mode_im = jnp.einsum("nfc,fnk->fkc", real_rows, vec_im, precision=precise) + jnp.einsum(
        "nfc,fnk->fkc", imag_rows, vec_re, precision=precise
    )
    return (mode_re, mode_im)


def body(snapshots, weights, start):
    seg_len, components, points = snapshots.shape
    columns = components * points
    samples = snapshots.reshape(seg_len, columns)
    basis = dft_table(NF, seg_len)
    tm_count = lax.axis_size("tm")
    blocks = tm_count - 1
    later = shifted(samples, "tm", -1)
    window_rows = jnp.concatenate([samples, later], 0)
    spectrum = jnp.dot(basis, window_rows, precision=precise)
    arrived = lax.all_to_all(
        spectrum.reshape(1, 2, NF, columns), "tm", split_axis=2, concat_axis=0, tiled=True
    )
    spectra = arrived[:blocks]
    col_weights = jnp.tile(weights, components)
    total_points = points * lax.axis_size("space")
    gram_re, gram_im = gram_parts(spectra, col_weights, total_points)
    gram_re, gram_im = lax.psum((gram_re, gram_im), "space")
    vec_re, vec_im = subspace(gram_re, gram_im, start)
    mode_re, mode_im = project(spectra, vec_re, vec_im)
    partial_energy = (
        jnp.sum((mode_re * mode_re + mode_im * mode_im) * col_weights, axis=-1) / total_points
    )
    energy = lax.psum(partial_energy, "space")
    inverse = 1.0 / jnp.sqrt(energy + epsilon)
    mode_out = jnp.stack([mode_re, mode_im], 2) * inverse[:, :, None, None]
    freq_count = mode_out.shape[0]
    return (mode_out.reshape(freq_count, mode_out.shape[1], 2, components, points), energy)


def solution(mesh):
    in_specs = (P("tm", None, "space"), P("space"), P())
    out_specs = (P("tm", None, None, None, "space"), P("tm", None))
    return jax.shard_map(body, mesh=mesh, in_specs=in_specs, out_specs=out_specs, check_vma=False)
```

profile of v0, /device:TPU:0, one launch (start us, length us, event | category | flops | bytes accessed | tf_op | source)
XLA Modules:
  0.0 132.0 jit_solution(17040012056975748923)
XLA Ops:
  0.6 1.9 %copy.460 = f32[256,3,512]{0,2,1:T(8,128)S(1)} copy(f32[256,3,512]{2,0,1:T(8,128)} %param.3) | data formatting | bytes 3145728 | tf_op args[0]
  2.5 1.3 collective-permute-start
  3.8 0.6 multiply_reduce_fusion.1
  5.2 0.5 multiply_multiply_fusion
  5.8 35.9 %collective-permute-done = f32[256,1536]{0,1:T(8,128)S(1)} collective-permute-done((f32[256,1536]{0,1:T(8,128)S(1)}, f32[256,1536]{0,1:T(8,128)S(1)}, u32[]{:S(2)}, u32[]{:S(2)}) %collective-permute-start) | collective-permute-done | bytes 1572896 | tf_op jit(solution)/shard_map/ppermute | solution.py:16
  41.7 3.3 %fusion = f32[128,1536]{1,0:T(8,128)S(1)} fusion(f32[256,1536]{0,1:T(8,128)S(1)} %collective-permute-done, f32[256,1536]{0,1:T(8,128)S(1)} %bitcast.878, f32[64,512]{1,0:T(8,128)S(1)} %get-tuple-element.722, f32[64,512]{1,0:T(8,128)S(1)} %get-tuple-element.723), kind=kOutput, calls=%fused_computation | convolution fusion | flops 1208811520 | bytes 4194304 | tf_op jit(solution)/shard_map/dot_general | solution.py:107
  45.1 1.5 %copy.461 = f32[1,2,64,1536]{3,1,0,2:T(2,128)} copy(f32[1,2,64,1536]{3,2,1,0:T(8,128)S(1)} %bitcast.879) | data formatting | bytes 1572864 | tf_op jit(solution)/shard_map/reshape | solution.py:109
  46.6 7.9 %all-to-all-start = ((f32[1,2,64,1536]{3,1,0,2:T(2,128)}), f32[1,2,64,1536]{3,1,0,2:T(2,128)S(1)}, u32[]{:S(2)}, u32[]{:S(2)}) async-start(f32[1,2,64,1536]{3,1,0,2:T(2,128)} %copy.461), calls=%async_computation | async-start | bytes 1572864 | tf_op jit(solution)/shard_map/all_to_all | solution.py:108
  54.5 18.8 %all-to-all-done = f32[1,2,64,1536]{3,1,0,2:T(2,128)S(1)} async-done(((f32[1,2,64,1536]{3,1,0,2:T(2,128)}), f32[1,2,64,1536]{3,1,0,2:T(2,128)S(1)}, u32[]{:S(2)}, u32[]{:S(2)}) %all-to-all-start) | async-done | bytes 786464 | tf_op jit(solution)/shard_map/all_to_all | solution.py:108
  73.4 0.5 copy.724
  73.9 3.4 %convolution_bitcast_fusion = f32[4,2,15,2,15]{2,4,1,3,0:T(8,128)S(1)} fusion(f32[16,1,2,4,1536]{4,0,2,3,1:T(8,128)S(1)} %bitcast.876, f32[1536]{0:T(1024)S(1)} %mul.8264), kind=kOutput, calls=%fused_computation.6 | convolution fusion | flops 66539520 | bytes 1595456 | tf_op jit(solution)/shard_map/nrfc,msfc->frnsm/dot_general | solution.py:32
  77.3 3.8 %all-reduce = (f32[4,15,15]{1,2,0:T(8,128)S(1)}, f32[4,15,15]{1,2,0:T(8,128)S(1)}) all-reduce(f32[4,15,15]{1,2,0:T(8,128)S(1)} %get-tuple-element.477, f32[4,15,15]{1,2,0:T(8,128)S(1)} %get-tuple-element.476), channel_id=1, replica_groups=mesh['tm'=16,'space'=2] {'space'}, use_global_device_ids=true, to_apply=%region_1.2 | all-reduce | flops 1800 | bytes 14400 | tf_op jit(solution)/shard_map/psum | solution.py:115
  81.2 0.2 fusion.24
  81.4 0.2 convolution_subtract_fusion.8
  81.6 0.2 convolution_add_fusion.8
  81.9 0.2 add_reduce_fusion.270
  82.1 0.2 add_reduce_fusion.269
  82.3 0.2 add_reduce_fusion.268
  86.9 0.2 fusion.65
  87.1 0.2 convolution_subtract_fusion.7
  87.3 0.2 convolution_add_fusion.7
  87.6 0.2 add_reduce_fusion.260
  87.7 0.2 add_reduce_fusion.259
  87.9 0.2 add_reduce_fusion.258
  92.6 0.2 fusion.67
  92.7 0.2 convolution_subtract_fusion.6
  92.9 0.2 convolution_add_fusion.6
  93.2 0.2 add_reduce_fusion.250
  93.4 0.2 add_reduce_fusion.249
  93.6 0.2 add_reduce_fusion.248
  98.0 0.2 fusion.68
  98.4 0.2 convolution_subtract_fusion.5
  98.6 0.2 convolution_add_fusion.5
  98.9 0.2 add_reduce_fusion.240
  99.1 0.2 add_reduce_fusion.239
  99.2 0.2 add_reduce_fusion.238
  104.0 0.2 convolution_subtract_fusion.4
  104.2 0.2 convolution_add_fusion.4
  104.5 0.2 add_reduce_fusion.230
  104.7 0.2 add_reduce_fusion.229
  104.9 0.2 add_reduce_fusion.228
  109.7 0.2 convolution_subtract_fusion.3
  109.9 0.2 convolution_add_fusion.3
  110.2 0.2 add_reduce_fusion.220
  110.4 0.2 add_reduce_fusion.219
  110.6 0.2 add_reduce_fusion.218
  115.6 0.2 convolution_subtract_fusion.2
  115.8 0.2 convolution_add_fusion.2
  116.1 0.2 add_reduce_fusion.210
  116.2 0.2 add_reduce_fusion.209
  116.4 0.2 add_reduce_fusion.208
  121.2 0.2 convolution_subtract_fusion.1
  121.4 0.2 convolution_add_fusion.1
  121.7 0.2 add_reduce_fusion.200
  121.9 0.2 add_reduce_fusion.199
  122.1 0.2 add_reduce_fusion.198
  126.6 0.3 fusion.9
  126.9 0.3 fusion.10
  127.2 0.3 convolution_subtract_fusion
  127.6 0.4 multiply_reduce_fusion
  128.0 0.2 copy.688
  128.2 2.5 %psum.23 = f32[4,8]{1,0:T(4,128)S(1)} all-reduce(f32[4,8]{1,0:T(4,128)S(1)} %broadcast_multiply_fusion), channel_id=1, replica_groups=mesh['tm'=16,'space'=2] {'space'}, use_global_device_ids=true, to_apply=%region_484.485 | all-reduce | flops 32 | bytes 256 | tf_op jit(solution)/shard_map/psum | solution.py:121
  130.7 0.2 copy.687
  130.9 1.1 maximum_multiply_fusion
  (555 shorter events, 36.0 us)
Async XLA Ops:
  2.5 39.2 %collective-permute-start = (f32[256,1536]{0,1:T(8,128)S(1)}, f32[256,1536]{0,1:T(8,128)S(1)}, u32[]{:S(2)}, u32[]{:S(2)}) collective-permute-start(f32[256,1536]{0,1:T(8,128)S(1)} %bitcast.877), channel_id=1, source_target_pairs={{2,0},{4,2},{6,4},{8,6},{10,8},{12,10},{14,12},{16,14},{18,16},{20... | collective-permute-start | bytes 4718600 | tf_op jit(solution)/shard_map/ppermute | solution.py:16
  45.1 9.4 %copy-start.2 = (f32[512]{0:T(512)S(1)}, f32[512]{0:T(512)}, u32[]{:S(2)}) copy-start(f32[512]{0:T(512)} %param.4) | copy-start | bytes 6148
  45.1 9.4 %copy-start = (f32[2,15,8]{1,2,0:T(8,128)S(1)}, f32[2,15,8]{1,2,0:T(8,128)}, u32[]{:S(2)}) copy-start(f32[2,15,8]{1,2,0:T(8,128)} %param.5) | copy-start | bytes 2884
  46.6 26.8 %all-to-all-start = ((f32[1,2,64,1536]{3,1,0,2:T(2,128)}), f32[1,2,64,1536]{3,1,0,2:T(2,128)S(1)}, u32[]{:S(2)}, u32[]{:S(2)}) async-start(f32[1,2,64,1536]{3,1,0,2:T(2,128)} %copy.461), calls=%async_computation | async-start | bytes 1572864 | tf_op jit(solution)/shard_map/all_to_all | solution.py:108
  130.7 1.3 %copy-start.1 = (f32[4,8]{1,0:T(4,128)}, f32[4,8]{1,0:T(4,128)S(1)}, u32[]{:S(2)}) copy-start(f32[4,8]{1,0:T(4,128)S(1)} %psum.23) | copy-start | bytes 388
where the time goes:
time: 132 us
  waiting for transfers between devices  54.8 us (42%)
  other arithmetic  38.5 us (29%)
  matrix products  13.4 us (10%)
  starting transfers between devices  9.18 us (7%)
  local copies, waits for them, and re-layouts  6.57 us (5%)
  blocking collectives  6.25 us (5%)
  between operations  3.29 us (2%)
    ppermute x1, waiting for transfers between devices, shifted(): return lax.ppermute(block, axis, route)  35.9 us
    all_to_all x1, waiting for transfers between devices, body(): lax.all_to_all(spectrum.reshape(1, 2, NF, columns), 'tm', split_axis=2, c...  18.8 us
    reduce_sum x112, other arithmetic, orthonormal(): jnp.sum(prev_re * part_re[..., None] + prev_im * part_im[..., None], axis=1)  13 us
    reduce_sum x96, other arithmetic, orthonormal(): jnp.sum(prev_re * coef_re[:, None, :] - prev_im * coef_im[:, None, :], ax...  9.33 us
    reduce_sum x64, other arithmetic, orthonormal(): jnp.sum(part_re * part_re + part_im * part_im, axis=1) + epsilon  8.27 us
    all_to_all x1, starting transfers between devices, body(): lax.all_to_all(spectrum.reshape(1, 2, NF, columns), 'tm', split_axis=2, c...  7.89 us
    mul x56, other arithmetic, orthonormal(): cols_re.append(part_re * inverse[:, None])  4.27 us
    psum x1, blocking collectives, body(): gram_re, gram_im = lax.psum((gram_re, gram_im), 'space')  3.78 us
  transfers between devices with their start and end apart: 2, of which 2 were waited for; matrix products, arithmetic and copies ran while one was open for 1% of the time, Pallas kernels for 0%

commit v1 on v0

--- a/solution.py
+++ b/solution.py
@@ -105,8 +105,14 @@
     later = shifted(samples, "tm", -1)
     window_rows = jnp.concatenate([samples, later], 0)
     spectrum = jnp.dot(basis, window_rows, precision=precise)
-    arrived = lax.all_to_all(
-        spectrum.reshape(1, 2, NF, columns), "tm", split_axis=2, concat_axis=0, tiled=True
+    arrived = jnp.concatenate(
+        lax.all_to_all(
+            jnp.stack(jnp.split(spectrum.reshape(1, 2, NF, columns), lax.axis_size("tm"), axis=2)),
+            "tm",
+            0,
+            0,
+        ),
+        axis=0,
     )
     spectra = arrived[:blocks]
     col_weights = jnp.tile(weights, components)

time: 132 us -> 142 us (1.076)
  local copies, waits for them, and re-layouts: 6.57 us -> 15.4 us
    unnamed x7 -> x23, local copies, waits for them, and re-layouts: 1.89 us -> 11.9 us
    reshape x1 -> x0, local copies, waits for them, and re-layouts: 1.48 us -> none  [body(): spectrum.reshape(1, 2, NF, columns)]
where the time goes in v1:
time: 142 us; the launch traced here: 141 us
  waiting for transfers between devices  54.8 us (39%)
  other arithmetic  38.5 us (27%)
  local copies, waits for them, and re-layouts  15.4 us (11%)
  matrix products  13.8 us (10%)
  starting transfers between devices  9.18 us (6%)
  blocking collectives  6.25 us (4%)
  between operations  3.3 us (2%)
    ppermute x1, waiting for transfers between devices, shifted(): return lax.ppermute(block, axis, route)  35.9 us
    all_to_all x1, waiting for transfers between devices, body(): lax.all_to_all(jnp.stack(jnp.split(spectrum.reshape(1, 2, NF, columns), l...  18.8 us
    reduce_sum x112, other arithmetic, orthonormal(): jnp.sum(prev_re * part_re[..., None] + prev_im * part_im[..., None], axis=1)  13 us
    unnamed x23, local copies, waits for them, and re-layouts  11.9 us
    reduce_sum x96, other arithmetic, orthonormal(): jnp.sum(prev_re * coef_re[:, None, :] - prev_im * coef_im[:, None, :], ax...  9.33 us
    reduce_sum x64, other arithmetic, orthonormal(): jnp.sum(part_re * part_re + part_im * part_im, axis=1) + epsilon  8.27 us
    all_to_all x1, starting transfers between devices, body(): lax.all_to_all(jnp.stack(jnp.split(spectrum.reshape(1, 2, NF, columns), l...  7.89 us
    mul x56, other arithmetic, orthonormal(): cols_re.append(part_re * inverse[:, None])  4.27 us
  transfers between devices with their start and end apart: 2, of which 2 were waited for; matrix products, arithmetic and copies ran while one was open for 1% of the time, Pallas kernels for 0%

profile of v1, /device:TPU:0, one launch (start us, length us, event | category | flops | bytes accessed | tf_op | source)
XLA Modules:
  0.0 141.3 jit_solution(1799427774813178125)
XLA Ops:
  0.6 1.9 %copy.490 = f32[256,3,512]{0,2,1:T(8,128)S(1)} copy(f32[256,3,512]{2,0,1:T(8,128)} %param.3) | data formatting | bytes 3145728 | tf_op args[0]
  2.5 1.3 collective-permute-start
  3.8 0.6 multiply_reduce_fusion.1
  5.2 0.5 multiply_multiply_fusion
  5.8 35.9 %collective-permute-done = f32[256,1536]{0,1:T(8,128)S(1)} collective-permute-done((f32[256,1536]{0,1:T(8,128)S(1)}, f32[256,1536]{0,1:T(8,128)S(1)}, u32[]{:S(2)}, u32[]{:S(2)}) %collective-permute-start) | collective-permute-done | bytes 1572896 | tf_op jit(solution)/shard_map/ppermute | solution.py:16
  41.7 3.3 %fusion = f32[128,1536]{1,0:T(8,128)S(1)} fusion(f32[256,1536]{0,1:T(8,128)S(1)} %collective-permute-done, f32[256,1536]{0,1:T(8,128)S(1)} %bitcast.941, f32[64,512]{1,0:T(8,128)S(1)} %get-tuple-element.738, f32[64,512]{1,0:T(8,128)S(1)} %get-tuple-element.739), kind=kOutput, calls=%fused_computation | convolution fusion | flops 1208811520 | bytes 4194304 | tf_op jit(solution)/shard_map/dot_general | solution.py:107
  45.2 0.6 fusion.35
  45.9 0.6 fusion.34
  46.5 0.6 fusion.33
  47.2 0.6 fusion.32
  47.8 0.6 fusion.31
  48.4 0.6 fusion.30
  49.1 0.6 fusion.29
  49.7 0.6 fusion.28
  50.4 0.6 fusion.27
  51.0 0.6 fusion.26
  51.6 0.6 fusion.25
  52.3 0.6 fusion.24
  52.9 0.6 fusion.23
  53.6 0.6 fusion.22
  54.2 0.6 fusion.21
  54.8 0.6 fusion.20
  55.5 7.9 %all-to-all-start = ((f32[16,1,2,4,1536]{4,2,3,1,0:T(2,128)}), f32[16,1,2,4,1536]{4,2,3,1,0:T(2,128)S(1)}, u32[]{:S(2)}, u32[]{:S(2)}) async-start(f32[16,1,2,4,1536]{4,2,3,1,0:T(2,128)} %fusion.20), calls=%async_computation | async-start | bytes 1572864 | tf_op jit(solution)/shard_map/all_to_all | solution.py:109
  63.4 18.8 %all-to-all-done = f32[16,1,2,4,1536]{4,2,3,1,0:T(2,128)S(1)} async-done(((f32[16,1,2,4,1536]{4,2,3,1,0:T(2,128)}), f32[16,1,2,4,1536]{4,2,3,1,0:T(2,128)S(1)}, u32[]{:S(2)}, u32[]{:S(2)}) %all-to-all-start) | async-done | bytes 786464 | tf_op jit(solution)/shard_map/all_to_all | solution.py:109
  82.3 0.4 copy.841
  82.8 3.8 %convolution_bitcast_fusion = f32[4,2,15,2,15]{2,4,1,3,0:T(8,128)S(1)} fusion(f32[15,1,2,4,1536]{4,2,3,1,0:T(2,128)S(1)} %slice.552, f32[1536]{0:T(1024)S(1)} %mul.8264), kind=kOutput, calls=%fused_computation.6 | convolution fusion | flops 66539520 | bytes 757824 | tf_op jit(solution)/shard_map/nrfc,msfc->frnsm/dot_general | solution.py:32
  86.5 3.8 %all-reduce = (f32[4,15,15]{1,2,0:T(8,128)S(1)}, f32[4,15,15]{1,2,0:T(8,128)S(1)}) all-reduce(f32[4,15,15]{1,2,0:T(8,128)S(1)} %get-tuple-element.493, f32[4,15,15]{1,2,0:T(8,128)S(1)} %get-tuple-element.492), channel_id=1, replica_groups=mesh['tm'=16,'space'=2] {'space'}, use_global_device_ids=true, to_apply=%region_1.2 | all-reduce | flops 1800 | bytes 14400 | tf_op jit(solution)/shard_map/psum | solution.py:121
  90.7 0.2 convolution_subtract_fusion.8
  91.1 0.2 add_reduce_fusion.270
  91.3 0.2 add_reduce_fusion.269
  91.5 0.2 add_reduce_fusion.268
  96.8 0.2 add_reduce_fusion.260
  97.0 0.2 add_reduce_fusion.259
  97.2 0.2 add_reduce_fusion.258
  102.0 0.2 convolution_subtract_fusion.6
  102.5 0.2 add_reduce_fusion.250
  102.6 0.2 add_reduce_fusion.249
  102.8 0.2 add_reduce_fusion.248
  107.6 0.2 convolution_subtract_fusion.5
  108.1 0.2 add_reduce_fusion.240
  108.3 0.2 add_reduce_fusion.239
  108.5 0.2 add_reduce_fusion.238
  113.3 0.2 convolution_subtract_fusion.4
  113.8 0.2 add_reduce_fusion.230
  114.0 0.2 add_reduce_fusion.229
  114.2 0.2 add_reduce_fusion.228
  119.0 0.2 convolution_subtract_fusion.3
  119.4 0.2 add_reduce_fusion.220
  119.6 0.2 add_reduce_fusion.219
  119.8 0.2 add_reduce_fusion.218
  125.3 0.2 add_reduce_fusion.210
  125.5 0.2 add_reduce_fusion.209
  125.7 0.2 add_reduce_fusion.208
  131.0 0.2 add_reduce_fusion.200
  131.2 0.2 add_reduce_fusion.199
  131.3 0.2 add_reduce_fusion.198
  135.8 0.3 fusion.9
  136.1 0.3 fusion.10
  136.5 0.3 convolution_subtract_fusion
  136.8 0.4 multiply_reduce_fusion
  137.2 0.2 copy.733
  137.5 2.5 %psum.23 = f32[4,8]{1,0:T(4,128)S(1)} all-reduce(f32[4,8]{1,0:T(4,128)S(1)} %broadcast_multiply_fusion), channel_id=1, replica_groups=mesh['tm'=16,'space'=2] {'space'}, use_global_device_ids=true, to_apply=%region_484.485 | all-reduce | flops 32 | bytes 256 | tf_op jit(solution)/shard_map/psum | solution.py:127
  139.9 0.2 copy.732
  140.2 1.1 maximum_multiply_fusion
  (571 shorter events, 38.6 us)
Async XLA Ops:
  2.5 39.2 %collective-permute-start = (f32[256,1536]{0,1:T(8,128)S(1)}, f32[256,1536]{0,1:T(8,128)S(1)}, u32[]{:S(2)}, u32[]{:S(2)}) collective-permute-start(f32[256,1536]{0,1:T(8,128)S(1)} %bitcast.940), channel_id=1, source_target_pairs={{2,0},{4,2},{6,4},{8,6},{10,8},{12,10},{14,12},{16,14},{18,16},{20... | collective-permute-start | bytes 4718600 | tf_op jit(solution)/shard_map/ppermute | solution.py:16
  45.2 18.2 %copy-start.2 = (f32[512]{0:T(512)S(1)}, f32[512]{0:T(512)}, u32[]{:S(2)}) copy-start(f32[512]{0:T(512)} %param.4) | copy-start | bytes 6148
  45.9 17.5 %copy-start = (f32[2,15,8]{1,2,0:T(8,128)S(1)}, f32[2,15,8]{1,2,0:T(8,128)}, u32[]{:S(2)}) copy-start(f32[2,15,8]{1,2,0:T(8,128)} %param.5) | copy-start | bytes 2884
  55.5 26.8 %all-to-all-start = ((f32[16,1,2,4,1536]{4,2,3,1,0:T(2,128)}), f32[16,1,2,4,1536]{4,2,3,1,0:T(2,128)S(1)}, u32[]{:S(2)}, u32[]{:S(2)}) async-start(f32[16,1,2,4,1536]{4,2,3,1,0:T(2,128)} %fusion.20), calls=%async_computation | async-start | bytes 1572864 | tf_op jit(solution)/shard_map/all_to_all | solution.py:109
  139.9 1.3 copy-start.1
